TPU v7x, 32 devices: a whole 2x2x4 slice. The times are simulated.
32 devices in a mesh: space: 8 (over z, y), vel: 4 (over x, core).
Axes of the slice: x: 2, y: 2, z: 4, core: 2. Of those that a mesh axis runs over, the one named last changes fastest.
Arguments:
- start_right: float32 [4096, 2048], P('vel', 'space'), may hold values from -6 to 6
- start_left: float32 [4096, 2048], P('vel', 'space'), may hold values from -6 to 6
- collision: bfloat16 [4096, 4096], P('vel'), may hold values from -0.125 to 0.125
- frequency: float32 [2048], P('space'), may hold values from 0.5 to 4
- volume: float32 [2048], P('space'), may hold values from 0.25 to 1
- face_neighbor: int32 [6, 2048], P(None, 'space'), may hold values from 0 to 767, as said below
- face_area: float32 [6, 2048], P(None, 'space'), as said below
- send_slot: int32 [4, 1024], P(None, 'space'), may hold values from 0 to 255, as said below
Outputs:
- right_basis: float32 [5, 4096, 2048], P(None, 'vel', 'space')
- left_basis: float32 [5, 4096, 2048], P(None, 'vel', 'space')
- right_hess: float32 [5, 4], replicated
- left_hess: float32 [5, 4], replicated
- cross_gram: float32 [5, 5], replicated
Inputs may be any that keep to these rules, and one draw needn't show every extreme that they name: `face_neighbor`: faces of a cell are ordered -x, +x, -y, +y, -z, +z. A value below 256 is a slot of the same block; a value 256 + g * 128 + k names entry k of what the block at offset (-2, 2, -1, 1)[g] provides in direction g. Every face of a cell and the face of the cell it reads form a mirrored pair. `face_area`: mirrored faces have equal areas; faces on the outer boundary of the domain have area 0, and so have faces across which face_neighbor points to no block. `send_slot`: entry (g, b * 128 + k) is a slot of block b: the cell that fills entry k of direction g for the block at offset -(-2, 2, -1, 1)[g] from b.
All inputs are finite; a program needn't handle non-finite values.
Results may differ from a plain program's by a relative error of at most 0.014.
Values may be sent and summed in bfloat16 or wider, within the bound.
A program may use at most 192 MiB of HBM per device.

v0:
```python
import jax
import jax.numpy as jnp
from jax import lax
from jax.sharding import PartitionSpec as P

NV = 16
ITERS = 4


EPSILON = 1e-06


def from_behind(block, axis, distance):
    devices = range(lax.axis_size(axis))
    route = [(i - distance, i) for i in devices if i - distance in devices]
    return lax.ppermute(block, axis, route)


def face_speeds(velocity_ids):
    along_x = velocity_ids // (NV * NV)
    along_y = velocity_ids // NV % NV
    along_z = velocity_ids % NV
    centre = (NV - 1) / 2.0
    spacing = 6.0 / NV
    speed_x = (along_x.astype(jnp.float32) - centre) * spacing
    speed_y = (along_y.astype(jnp.float32) - centre) * spacing
    speed_z = (along_z.astype(jnp.float32) - centre) * spacing
    return [-speed_x, speed_x, -speed_y, speed_y, -speed_z, speed_z]


def per_device(
    start_right, start_left, collision, frequency, volume, face_neighbor, face_area, send_slot
):
    vel_rows, cell_count = start_right.shape
    row_blocks = lax.axis_size("space") // 4
    offsets = [row_blocks, -row_blocks, 1, -1]
    velocity_ids = lax.axis_index("vel") * vel_rows + jnp.arange(vel_rows, dtype=jnp.int32)
    speeds = face_speeds(velocity_ids)
    inv_vol = 1.0 / volume
    halo_vol = []
    for direction in range(4):
        sent_vol = jnp.take(inv_vol, send_slot[direction])
        halo_vol.append(from_behind(sent_vol, "space", offsets[direction]))
    inv_ext = jnp.concatenate([inv_vol] + halo_vol)
    beside_inv = [jnp.take(inv_ext, face_neighbor[facing]) for facing in range(6)]
    squares = lax.psum(
        (jnp.sum(start_right * start_right), jnp.sum(start_left * start_left)), ("space", "vel")
    )
    right_list = [start_right / jnp.sqrt(squares[0] + EPSILON)]
    left_list = [start_left / jnp.sqrt(squares[1] + EPSILON)]
    right_hess = jnp.zeros((ITERS + 1, ITERS), jnp.float32)
    left_hess = jnp.zeros((ITERS + 1, ITERS), jnp.float32)
    for column_idx in range(ITERS):
        right_w = right_list[column_idx].astype(jnp.bfloat16)
        left_w = left_list[column_idx].astype(jnp.bfloat16)
        right_got = []
        left_got = []
        for extended_direction in range(4):
            message = jnp.stack(
                [
                    jnp.take(right_w, send_slot[extended_direction], axis=1),
                    jnp.take(left_w, send_slot[extended_direction], axis=1),
                ]
            )
            arrived = from_behind(message, "space", offsets[extended_direction])
            right_got.append(arrived[0])
            left_got.append(arrived[1])
        right_ext = jnp.concatenate([right_w] + right_got, axis=1)
        left_ext = jnp.concatenate([left_w] + left_got, axis=1)
        right_wide = right_w.astype(jnp.float32)
        left_wide = left_w.astype(jnp.float32)
        forward = jnp.zeros((vel_rows, cell_count), jnp.float32)
        adjoint = jnp.zeros((vel_rows, cell_count), jnp.float32)
        for transport_facing in range(6):
            speed_col = speeds[transport_facing][:, None]
            face_wt = face_area[transport_facing]
            beside_right = jnp.take(right_ext, face_neighbor[transport_facing], axis=1).astype(
                jnp.float32
            )
            beside_left = jnp.take(left_ext, face_neighbor[transport_facing], axis=1).astype(
                jnp.float32
            )
            forward = forward + face_wt * inv_vol * (
                jnp.maximum(speed_col, 0.0) * right_wide
                + jnp.minimum(speed_col, 0.0) * beside_right
            )
            adjoint = adjoint + face_wt * (
                jnp.maximum(speed_col, 0.0) * left_wide * inv_vol
                + jnp.minimum(-speed_col, 0.0) * beside_left * beside_inv[transport_facing]
            )
        forward, adjoint = (forward, adjoint)
        right_new = forward + frequency * lax.psum_scatter(
            lax.dot_general(
                collision, right_w, (((0,), (0,)), ((), ())), preferred_element_type=jnp.float32
            ).astype(jnp.bfloat16),
            "vel",
            scatter_dimension=0,
            tiled=True,
        ).astype(jnp.float32)
        left_new = adjoint + frequency * jnp.dot(
            collision,
            lax.all_gather(left_w, "vel", axis=0, tiled=True),
            preferred_element_type=jnp.float32,
        )
        dots_right = jnp.stack([jnp.sum(vector * right_new) for vector in right_list])
        dots_left = jnp.stack([jnp.sum(vector * left_new) for vector in left_list])
        right_coef, left_coef, right_raw, left_raw = lax.psum(
            (dots_right, dots_left, jnp.sum(right_new * right_new), jnp.sum(left_new * left_new)),
            ("space", "vel"),
        )
        for older in range(column_idx + 1):
            right_new = right_new - right_coef[older] * right_list[older]
            left_new = left_new - left_coef[older] * left_list[older]
        right_norm = jnp.sqrt(right_raw - jnp.sum(right_coef * right_coef) + EPSILON)
        left_norm = jnp.sqrt(left_raw - jnp.sum(left_coef * left_coef) + EPSILON)
        right_hess = (
            right_hess.at[: column_idx + 1, column_idx]
            .set(right_coef)
            .at[column_idx + 1, column_idx]
            .set(right_norm)
        )
        left_hess = (
            left_hess.at[: column_idx + 1, column_idx]
            .set(left_coef)
            .at[column_idx + 1, column_idx]
            .set(left_norm)
        )
        right_list.append(right_new / right_norm)
        left_list.append(left_new / left_norm)
    right_basis = jnp.stack(right_list)
    left_basis = jnp.stack(left_list)
    cross_local = jnp.einsum(
        "ivc,kvc->ik", left_basis, right_basis, precision=lax.Precision.HIGHEST
    )
    cross_gram = lax.psum(cross_local, ("space", "vel"))
    return (right_basis, left_basis, right_hess, left_hess, cross_gram)


def solution(mesh):
    placed = (
        P("vel", "space"),
        P("vel", "space"),
        P("vel", None),
        P("space"),
        P("space"),
        P(None, "space"),
        P(None, "space"),
        P(None, "space"),
    )
    return jax.shard_map(
        per_device,
        mesh=mesh,
        in_specs=placed,
        out_specs=(P(None, "vel", "space"), P(None, "vel", "space"), P(), P(), P()),
        check_vma=False,
    )
```

profile of v0, /device:TPU:0, one launch (start us, length us, event | category | flops | bytes accessed | tf_op | source)
XLA Modules:
  0.0 865.7 jit_solution(7090446399949832883)
XLA Ops:
  11.4 42.2 %all-reduce.6 = (f32[]{:T(128)}, f32[]{:T(128)}) all-reduce(f32[]{:T(128)} %get-tuple-element.425, f32[]{:T(128)} %get-tuple-element.424), channel_id=1, replica_groups=mesh['space'=8,'vel'=4] {'space','vel'}, use_global_device_ids=true, to_apply=%region_1.2 | all-reduce | flops 2 | bytes 16 | tf_op jit(solution)/shard_map/psum | solution.py:46
  86.0 5.2 collective-permute-start.2
  105.6 7.2 fusion.3
  172.0 13.9 %multiply_reduce_fusion.25 = (f32[]{:T(128)}, f32[]{:T(128)}, f32[1024,256]{0,1:T(8,128)}) fusion(f32[1024,256]{0,1:T(8,128)} %copy-done.19, f32[]{:T(128)S(6)} %sqrt.31, bf16[4096,256]{0,1:T(8,128)(2,1)} %all-gather.5.cloned.1.call-done, bf16[1024,4096]{1,0:T(8,128)(2,1)} %param.50, f32[256]{0:T(256)S(1)} %copy-done.44, f32[256]{0:T(256)S(1)} %get-tuple-element.291, ...), kind=kOutput, calls=%fused_computation.366 | convolution fusion | flops 2163474432 | bytes 16317964 | tf_op jit(solution)/shard_map/dot_general | solution.py:100
  185.9 5.5 multiply_reduce_fusion.27
  191.4 41.0 %all-reduce.5 = (f32[]{:T(128)}, f32[1]{0:T(128)}, f32[]{:T(128)}, f32[1]{0:T(128)}) all-reduce(f32[]{:T(128)} %get-tuple-element.238, f32[1]{0:T(128)} %bitcast.44, f32[]{:T(128)} %get-tuple-element.236, f32[1]{0:T(128)} %bitcast.61), channel_id=1, replica_groups=mesh['space'=8,'vel'=4] {'space','vel'}, use_global_device_ids=true, to_apply=%region_8.11 | all-reduce | flops 4 | bytes 32 | tf_op jit(solution)/shard_map/psum | solution.py:107
  245.7 7.7 fusion.4
  288.3 6.0 collective-permute-done.8
  294.3 7.5 collective-permute-done.9
  326.0 14.0 %multiply_reduce_fusion.20 = (f32[]{:T(128)}, f32[]{:T(128)}, f32[]{:T(128)}, f32[1024,256]{0,1:T(8,128)}) fusion(f32[1024,256]{0,1:T(8,128)} %copy-done.19, f32[]{:T(128)S(6)} %sqrt.31, f32[1024,256]{0,1:T(8,128)} %copy-done.24, bf16[4096,256]{0,1:T(8,128)(2,1)} %all-gather.7.cloned.1.call-done, bf16[1024,4096]{1,0:T(8,128)(2,1)} %param.50, ...), kind=kOutput, calls=%fused_computation.359 | convolution fusion | flops 2163998720 | bytes 17366544 | tf_op jit(solution)/shard_map/dot_general | solution.py:100
  341.5 5.5 multiply_reduce_fusion.23
  348.4 46.9 %all-reduce.4 = (f32[]{:T(128)}, f32[2]{0:T(128)S(1)}, f32[]{:T(128)}, f32[2]{0:T(128)S(1)}) all-reduce(f32[]{:T(128)} %get-tuple-element.233, f32[2]{0:T(128)S(1)} %pad_maximum_fusion.16, f32[]{:T(128)} %get-tuple-element.230, f32[2]{0:T(128)S(1)} %pad_maximum_fusion.17), channel_id=1, replica_groups=mesh['space'=8,'vel'=4] {'space','vel'}, use_global_device_ids=true, to_apply=%region_18.23 | all-reduce | flops 6 | bytes 48 | tf_op jit(solution)/shard_map/psum | solution.py:107
  413.8 7.1 fusion.5
  457.2 6.8 collective-permute-done.12
  464.1 6.8 collective-permute-done.13
  494.4 14.6 %multiply_reduce_fusion.13 = (f32[]{:T(128)}, f32[]{:T(128)}, f32[]{:T(128)}, f32[]{:T(128)}, f32[1024,256]{0,1:T(8,128)}) fusion(f32[1024,256]{0,1:T(8,128)} %copy-done.19, f32[]{:T(128)S(6)} %sqrt.31, f32[1024,256]{0,1:T(8,128)} %copy-done.25, f32[1024,256]{0,1:T(8,128)} %copy-done.24, bf16[4096,256]{0,1:T(8,128)(2,1)} %all-gather.9.cloned.1.call-done, ...), kind=kOutput, calls=%fused_computation.350 | convolution fusion | flops 2164523008 | bytes 18415124 | tf_op jit(solution)/shard_map/dot_general | solution.py:100
  511.0 5.8 multiply_reduce_fusion.17
  518.9 47.9 %all-reduce.3 = (f32[]{:T(128)}, f32[3]{0:T(128)}, f32[]{:T(128)}, f32[3]{0:T(128)S(1)}) all-reduce(f32[]{:T(128)} %get-tuple-element.226, f32[3]{0:T(128)S(1)} %pad_maximum_fusion.18, f32[]{:T(128)} %get-tuple-element.222, f32[3]{0:T(128)S(1)} %pad_maximum_fusion.19), channel_id=1, replica_groups=mesh['space'=8,'vel'=4] {'space','vel'}, use_global_device_ids=true, to_apply=%region_32.37 | all-reduce | flops 8 | bytes 64 | tf_op jit(solution)/shard_map/psum | solution.py:107
  569.3 5.6 bitcast_dynamic-update-slice_fusion.1
  597.2 5.8 constant_dynamic-update-slice_fusion.7
  623.5 7.1 fusion.6
  632.6 5.8 collective-permute-start.18
  641.8 5.4 collective-permute-start.16
  685.0 14.7 %multiply_reduce_fusion.4 = (f32[]{:T(128)}, f32[]{:T(128)}, f32[]{:T(128)}, f32[]{:T(128)}, f32[]{:T(128)}, /*index=5*/f32[1024,256]{0,1:T(8,128)}) fusion(f32[1024,256]{0,1:T(8,128)} %copy-done.19, f32[]{:T(128)S(6)} %sqrt.31, f32[1024,256]{0,1:T(8,128)} %copy-done.27, f32[1024,256]{0,1:T(8,128)} %copy-done.25, f32[1024,256]{0,1:T(8,128)} %copy-done.24, ...), kind=kOutput, calls=%fused_computation.340 | convolution fusion | flops 2165047296 | bytes 19463704 | tf_op jit(solution)/shard_map/dot_general | solution.py:100
  702.4 6.2 multiply_reduce_fusion.9
  711.3 44.8 %all-reduce.2 = (f32[]{:T(128)}, f32[4]{0:T(128)S(1)}, f32[]{:T(128)}, f32[4]{0:T(128)S(1)}) all-reduce(f32[]{:T(128)} %get-tuple-element.217, f32[4]{0:T(128)S(1)} %pad_maximum_fusion.20, f32[]{:T(128)} %get-tuple-element.212, f32[4]{0:T(128)S(1)} %pad_maximum_fusion.21), channel_id=1, replica_groups=mesh['space'=8,'vel'=4] {'space','vel'}, use_global_device_ids=true, to_apply=%region_48.53 | all-reduce | flops 10 | bytes 80 | tf_op jit(solution)/shard_map/psum | solution.py:107
  761.2 6.5 bitcast_dynamic-update-slice_fusion
  767.7 6.0 copy.24
  773.7 5.9 bitcast_dynamic-update-slice_fusion.5
  779.7 25.0 %fusion.15 = f32[5,5]{1,0:T(8,128)S(1)} fusion(f32[5,1024,256]{1,2,0:T(8,128)} %bitcast_dynamic-update-slice_fusion.5, f32[5,1024,256]{1,2,0:T(8,128)S(1)} %copy-done.21), kind=kOutput, calls=%fused_computation.161 | convolution fusion | flops 78643200 | bytes 10485860 | tf_op jit(solution)/shard_map/ivc,kvc->ik/dot_general | solution.py:132
  804.6 5.9 copy.23
  810.5 39.7 %psum.151 = f32[5,5]{1,0:T(8,128)} all-reduce(f32[5,5]{1,0:T(8,128)S(1)} %fusion.15), channel_id=1, replica_groups=mesh['space'=8,'vel'=4] {'space','vel'}, use_global_device_ids=true, to_apply=%region_61.66 | all-reduce | flops 25 | bytes 200 | tf_op jit(solution)/shard_map/psum | solution.py:135
  (560 shorter events, 359.6 us)
Async XLA Ops:
  7.2 164.7 %all-gather.5.cloned.1.call-start = ((), (), s32[]{:S(2)}) async-start(), calls=%async_computation.5 | async-start | bytes 2621440 | tf_op jit(solution)/shard_map/all_gather | solution.py:102
  55.3 130.6 %reduce-scatter.5.cloned.1.call-start = ((), (), s32[]{:S(2)}) async-start(), calls=%async_computation.4 | async-start | bytes 2621440 | tf_op jit(solution)/shard_map/reduce_scatter | solution.py:92
  66.6 77.3 %collective-permute-start = (bf16[2,1024,128]{1,2,0:T(8,128)(2,1)}, bf16[2,1024,128]{1,2,0:T(8,128)(2,1)}, u32[]{:S(2)}, u32[]{:S(2)}) collective-permute-start(bf16[2,1024,128]{1,2,0:T(8,128)(2,1)} %pad_maximum_fusion), channel_id=1, source_target_pairs={{0,8},{4,12},{8,16},{12,20},{16,24},{20,28},{1,9},{5,13},{9,17},{1... | collective-permute-start | bytes 1572872 | tf_op jit(solution)/shard_map/ppermute | solution.py:16
  77.7 67.2 %collective-permute-start.1 = (bf16[2,1024,128]{1,2,0:T(8,128)(2,1)}, bf16[2,1024,128]{1,2,0:T(8,128)(2,1)}, u32[]{:S(2)}, u32[]{:S(2)}) collective-permute-start(bf16[2,1024,128]{1,2,0:T(8,128)(2,1)} %pad_maximum_fusion.1), channel_id=1, source_target_pairs={{8,0},{12,4},{16,8},{20,12},{24,16},{28,20},{9,1},{13,5},{17,9},{2... | collective-permute-start | bytes 1572872 | tf_op jit(solution)/shard_map/ppermute | solution.py:16
  86.0 60.0 %collective-permute-start.2 = (bf16[2,1024,128]{1,2,0:T(8,128)(2,1)}, bf16[2,1024,128]{1,2,0:T(8,128)(2,1)}, u32[]{:S(2)}, u32[]{:S(2)}) collective-permute-start(bf16[2,1024,128]{1,2,0:T(8,128)(2,1)} %pad_maximum_fusion.2), channel_id=1, source_target_pairs={{0,4},{4,8},{8,12},{12,16},{16,20},{20,24},{24,28},{1,5},{5,9},{9,... | collective-permute-start | bytes 1572872 | tf_op jit(solution)/shard_map/ppermute | solution.py:16
  98.2 48.9 %collective-permute-start.3 = (bf16[2,1024,128]{1,2,0:T(8,128)(2,1)}, bf16[2,1024,128]{1,2,0:T(8,128)(2,1)}, u32[]{:S(2)}, u32[]{:S(2)}) collective-permute-start(bf16[2,1024,128]{1,2,0:T(8,128)(2,1)} %pad_maximum_fusion.3), channel_id=1, source_target_pairs={{4,0},{8,4},{12,8},{16,12},{20,16},{24,20},{28,24},{5,1},{9,5},{13... | collective-permute-start | bytes 1572872 | tf_op jit(solution)/shard_map/ppermute | solution.py:16
  100.8 18.7 %collective-permute-start.4 = (f32[128]{0:T(128)S(1)}, f32[128]{0:T(128)S(1)}, u32[]{:S(2)}, u32[]{:S(2)}) collective-permute-start(f32[128]{0:T(128)S(1)} %broadcast_select_fusion.15), channel_id=1, source_target_pairs={{0,8},{4,12},{8,16},{12,20},{16,24},{20,28},{1,9},{5,13},{9,17},{1... | collective-permute-start | bytes 1544 | tf_op jit(solution)/shard_map/ppermute | solution.py:16
  112.8 213.0 %all-gather.7.cloned.1.call-start = ((), (), s32[]{:S(2)}) async-start(), calls=%async_computation.7 | async-start | bytes 2621440 | tf_op jit(solution)/shard_map/all_gather | solution.py:102
  119.4 52.5 %copy-start.77 = (f32[1,256]{1,0:T(1,128)}, f32[1,256]{1,0:T(1,128)S(1)}, u32[]{:S(2)}) copy-start(f32[1,256]{1,0:T(1,128)S(1)} %get-tuple-element.340) | copy-start | bytes 3076
  119.4 52.5 %copy-start.81 = (f32[1,256]{1,0:T(1,128)}, f32[1,256]{1,0:T(1,128)S(1)}, u32[]{:S(2)}) copy-start(f32[1,256]{1,0:T(1,128)S(1)} %get-tuple-element.341) | copy-start | bytes 3076
  119.4 52.5 %copy-start.85 = (f32[1,256]{1,0:T(1,128)}, f32[1,256]{1,0:T(1,128)S(1)}, u32[]{:S(2)}) copy-start(f32[1,256]{1,0:T(1,128)S(1)} %get-tuple-element.342) | copy-start | bytes 3076
  119.4 52.5 %copy-start.89 = (f32[1,256]{1,0:T(1,128)}, f32[1,256]{1,0:T(1,128)S(1)}, u32[]{:S(2)}) copy-start(f32[1,256]{1,0:T(1,128)S(1)} %get-tuple-element.343) | copy-start | bytes 3076
  119.5 5.4 collective-permute-start.5
  124.9 4.8 collective-permute-start.6
  129.7 5.7 collective-permute-start.7
  239.3 102.2 %reduce-scatter.7.cloned.1.call-start = ((), (), s32[]{:S(2)}) async-start(), calls=%async_computation.6 | async-start | bytes 2621440 | tf_op jit(solution)/shard_map/reduce_scatter | solution.py:92
  253.4 240.8 %all-gather.9.cloned.1.call-start = ((), (), s32[]{:S(2)}) async-start(), calls=%async_computation.9 | async-start | bytes 2621440 | tf_op jit(solution)/shard_map/all_gather | solution.py:102
  277.3 24.5 %collective-permute-start.10 = (bf16[2,1024,128]{1,2,0:T(8,128)(2,1)S(1)}, bf16[2,1024,128]{1,2,0:T(8,128)(2,1)S(1)}, u32[]{:S(2)}, u32[]{:S(2)}) collective-permute-start(bf16[2,1024,128]{1,2,0:T(8,128)(2,1)S(1)} %pad_maximum_fusion.6), channel_id=1, source_target_pairs={{0,4},{4,8},{8,12},{12,16},{16,20},{20,24},{24,28},{1,5},{5,9},{9,... | collective-permute-start | bytes 1572872 | tf_op jit(solution)/shard_map/ppermute | solution.py:16
  281.9 12.3 %collective-permute-start.8 = (bf16[2,1024,128]{1,2,0:T(8,128)(2,1)S(1)}, bf16[2,1024,128]{1,2,0:T(8,128)(2,1)S(1)}, u32[]{:S(2)}, u32[]{:S(2)}) collective-permute-start(bf16[2,1024,128]{1,2,0:T(8,128)(2,1)S(1)} %pad_maximum_fusion.4), channel_id=1, source_target_pairs={{0,8},{4,12},{8,16},{12,20},{16,24},{20,28},{1,9},{5,13},{9,17},{1... | collective-permute-start | bytes 1572872 | tf_op jit(solution)/shard_map/ppermute | solution.py:16
  285.0 16.8 %collective-permute-start.9 = (bf16[2,1024,128]{1,2,0:T(8,128)(2,1)S(1)}, bf16[2,1024,128]{1,2,0:T(8,128)(2,1)S(1)}, u32[]{:S(2)}, u32[]{:S(2)}) collective-permute-start(bf16[2,1024,128]{1,2,0:T(8,128)(2,1)S(1)} %pad_maximum_fusion.5), channel_id=1, source_target_pairs={{8,0},{12,4},{16,8},{20,12},{24,16},{28,20},{9,1},{13,5},{17,9},{2... | collective-permute-start | bytes 1572872 | tf_op jit(solution)/shard_map/ppermute | solution.py:16
  286.5 15.4 %collective-permute-start.11 = (bf16[2,1024,128]{1,2,0:T(8,128)(2,1)S(1)}, bf16[2,1024,128]{1,2,0:T(8,128)(2,1)S(1)}, u32[]{:S(2)}, u32[]{:S(2)}) collective-permute-start(bf16[2,1024,128]{1,2,0:T(8,128)(2,1)S(1)} %pad_maximum_fusion.7), channel_id=1, source_target_pairs={{4,0},{8,4},{12,8},{16,12},{20,16},{24,20},{28,24},{5,1},{9,5},{13... | collective-permute-start | bytes 1572872 | tf_op jit(solution)/shard_map/ppermute | solution.py:16
  404.4 106.6 %reduce-scatter.9.cloned.1.call-start = ((), (), s32[]{:S(2)}) async-start(), calls=%async_computation.8 | async-start | bytes 2621440 | tf_op jit(solution)/shard_map/reduce_scatter | solution.py:92
  420.9 264.0 %all-gather.11.cloned.1.call-start = ((), (), s32[]{:S(2)}) async-start(), calls=%async_computation.11 | async-start | bytes 2621440 | tf_op jit(solution)/shard_map/all_gather | solution.py:102
  446.0 24.9 %collective-permute-start.14 = (bf16[2,1024,128]{1,2,0:T(8,128)(2,1)S(1)}, bf16[2,1024,128]{1,2,0:T(8,128)(2,1)S(1)}, u32[]{:S(2)}, u32[]{:S(2)}) collective-permute-start(bf16[2,1024,128]{1,2,0:T(8,128)(2,1)S(1)} %pad_maximum_fusion.10), channel_id=1, source_target_pairs={{0,4},{4,8},{8,12},{12,16},{16,20},{20,24},{24,28},{1,5},{5,9},{9,... | collective-permute-start | bytes 1572872 | tf_op jit(solution)/shard_map/ppermute | solution.py:16
  450.8 13.3 %collective-permute-start.12 = (bf16[2,1024,128]{1,2,0:T(8,128)(2,1)S(1)}, bf16[2,1024,128]{1,2,0:T(8,128)(2,1)S(1)}, u32[]{:S(2)}, u32[]{:S(2)}) collective-permute-start(bf16[2,1024,128]{1,2,0:T(8,128)(2,1)S(1)} %pad_maximum_fusion.8), channel_id=1, source_target_pairs={{0,8},{4,12},{8,16},{12,20},{16,24},{20,28},{1,9},{5,13},{9,17},{1... | collective-permute-start | bytes 1572872 | tf_op jit(solution)/shard_map/ppermute | solution.py:16
  454.2 16.8 %collective-permute-start.13 = (bf16[2,1024,128]{1,2,0:T(8,128)(2,1)S(1)}, bf16[2,1024,128]{1,2,0:T(8,128)(2,1)S(1)}, u32[]{:S(2)}, u32[]{:S(2)}) collective-permute-start(bf16[2,1024,128]{1,2,0:T(8,128)(2,1)S(1)} %pad_maximum_fusion.9), channel_id=1, source_target_pairs={{8,0},{12,4},{16,8},{20,12},{24,16},{28,20},{9,1},{13,5},{17,9},{2... | collective-permute-start | bytes 1572872 | tf_op jit(solution)/shard_map/ppermute | solution.py:16
  455.7 15.4 %collective-permute-start.15 = (bf16[2,1024,128]{1,2,0:T(8,128)(2,1)S(1)}, bf16[2,1024,128]{1,2,0:T(8,128)(2,1)S(1)}, u32[]{:S(2)}, u32[]{:S(2)}) collective-permute-start(bf16[2,1024,128]{1,2,0:T(8,128)(2,1)S(1)} %pad_maximum_fusion.11), channel_id=1, source_target_pairs={{4,0},{8,4},{12,8},{16,12},{20,16},{24,20},{28,24},{5,1},{9,5},{13... | collective-permute-start | bytes 1572872 | tf_op jit(solution)/shard_map/ppermute | solution.py:16
  576.9 125.5 %reduce-scatter.11.cloned.1.call-start = ((), (), s32[]{:S(2)}) async-start(), calls=%async_computation.10 | async-start | bytes 2621440 | tf_op jit(solution)/shard_map/reduce_scatter | solution.py:92
  622.2 37.7 %collective-permute-start.19 = (bf16[2,1024,128]{1,2,0:T(8,128)(2,1)}, bf16[2,1024,128]{1,2,0:T(8,128)(2,1)}, u32[]{:S(2)}, u32[]{:S(2)}) collective-permute-start(bf16[2,1024,128]{1,2,0:T(8,128)(2,1)} %pad_maximum_fusion.15), channel_id=1, source_target_pairs={{4,0},{8,4},{12,8},{16,12},{20,16},{24,20},{28,24},{5,1},{9,5},{13... | collective-permute-start | bytes 1572872 | tf_op jit(solution)/shard_map/ppermute | solution.py:16
  632.6 26.2 %collective-permute-start.18 = (bf16[2,1024,128]{1,2,0:T(8,128)(2,1)}, bf16[2,1024,128]{1,2,0:T(8,128)(2,1)}, u32[]{:S(2)}, u32[]{:S(2)}) collective-permute-start(bf16[2,1024,128]{1,2,0:T(8,128)(2,1)} %pad_maximum_fusion.14), channel_id=1, source_target_pairs={{0,4},{4,8},{8,12},{12,16},{16,20},{20,24},{24,28},{1,5},{5,9},{9,... | collective-permute-start | bytes 1572872 | tf_op jit(solution)/shard_map/ppermute | solution.py:16
  639.4 18.3 %collective-permute-start.17 = (bf16[2,1024,128]{1,2,0:T(8,128)(2,1)}, bf16[2,1024,128]{1,2,0:T(8,128)(2,1)}, u32[]{:S(2)}, u32[]{:S(2)}) collective-permute-start(bf16[2,1024,128]{1,2,0:T(8,128)(2,1)} %pad_maximum_fusion.13), channel_id=1, source_target_pairs={{8,0},{12,4},{16,8},{20,12},{24,16},{28,20},{9,1},{13,5},{17,9},{2... | collective-permute-start | bytes 1572872 | tf_op jit(solution)/shard_map/ppermute | solution.py:16
  641.8 14.8 %collective-permute-start.16 = (bf16[2,1024,128]{1,2,0:T(8,128)(2,1)}, bf16[2,1024,128]{1,2,0:T(8,128)(2,1)}, u32[]{:S(2)}, u32[]{:S(2)}) collective-permute-start(bf16[2,1024,128]{1,2,0:T(8,128)(2,1)} %pad_maximum_fusion.12), channel_id=1, source_target_pairs={{0,8},{4,12},{8,16},{12,20},{16,24},{20,28},{1,9},{5,13},{9,17},{1... | collective-permute-start | bytes 1572872 | tf_op jit(solution)/shard_map/ppermute | solution.py:16
  (126 other events, 1099.2 us)
Sparse Core Ops, SparseCore 0:
  55.4 22.5 all-gather.4
  113.0 30.1 reduce-scatter.4
  239.4 23.3 all-gather.6
  265.9 31.4 reduce-scatter.6
  404.6 23.7 all-gather.8
  431.3 31.4 reduce-scatter.8
  577.0 23.6 all-gather.10
  630.7 33.9 reduce-scatter.10
where the time goes:
time: 878 us; the launch traced here: 866 us
  blocking collectives  263 us (30%)
  local copies, waits for them, and re-layouts  243 us (28%)
  other arithmetic  123 us (14%)
  matrix products  111 us (13%)
  starting transfers between devices  58.5 us (7%)
  waiting for transfers between devices  38.3 us (4%)
  between operations  30.1 us (3%)
    psum x4, blocking collectives, per_device(): lax.psum((dots_right, dots_left, jnp.sum(right_new * right_new), jnp.sum(...  181 us
    ppermute x20, starting transfers between devices, from_behind(): return lax.ppermute(block, axis, route)  57.7 us
    dot_general x4, matrix products, per_device(): jnp.dot(collision, lax.all_gather(left_w, 'vel', axis=0, tiled=True), pre...  57.2 us
    gather x24, local copies, waits for them, and re-layouts, per_device(): jnp.take(left_ext, face_neighbor[transport_facing], axis=1)  47.5 us
    gather x24, local copies, waits for them, and re-layouts, per_device(): jnp.take(right_ext, face_neighbor[transport_facing], axis=1)  46.6 us
    gather x16, local copies, waits for them, and re-layouts, per_device(): jnp.take(right_w, send_slot[extended_direction], axis=1)  43.8 us
    psum x1, blocking collectives, per_device(): lax.psum((jnp.sum(start_right * start_right), jnp.sum(start_left * start_...  42.2 us
    psum x1, blocking collectives, per_device(): cross_gram = lax.psum(cross_local, ('space', 'vel'))  39.7 us
  transfers between devices with their start and end apart: 28, of which 8 were waited for; matrix products, arithmetic and copies ran while one was open for 41% of the time, Pallas kernels for 0%

commit v1 on v0

v1 whole, which is shorter than its diff:
```python
import functools

import jax
import jax.numpy as jnp
from jax import lax
from jax.experimental import pallas as pl
from jax.experimental.pallas import tpu as pltpu
from jax.sharding import PartitionSpec as P

NV = 16
ITERS = 4
EPSILON = 1e-06
LANES = 128
CHUNK = 256
MESH = pl.DeviceIdType.MESH
F32 = jnp.float32
BF16 = jnp.bfloat16


def dot(a, b):
    return jnp.dot(a, b, preferred_element_type=F32)


def kernel(
    sizes, start_r, start_l, coll_hbm, freq_ref, vol_ref, fn_ref, fa_ref, ss_ref,
    right_out, left_out, rh_out, lh_out, gram_out,
    coll, coll_t, pr, ql, wr, wl, hsend, halo, pack, gather, ivp, area_l,
    diag, speed, part, rs_send, rs_got, rs_xsend, rs_xgot,
    red_own, red_vel, red_mid, red_space,
    in_sem, out_sem, ag_send, ag_recv, rs_ssem, rs_rsem, h_send, h_recv,
    v_send, v_recv, s_send, s_recv,
):
    n_space, n_vel, row_blocks = sizes
    _, rows, cells = pr.shape
    face = hsend.shape[2]
    half = rows // 2
    steps = rows // CHUNK
    space = lax.axis_index("space")
    vel = lax.axis_index("vel")
    chip, core = vel // 2, vel % 2
    near = chip * 2 + (1 - core)
    far = (1 - chip) * 2 + core
    diagonal = (1 - chip) * 2 + (1 - core)
    offsets = [row_blocks, -row_blocks, 1, -1]

    def at(c):
        return pl.ds(pl.multiple_of(c * CHUNK, CHUNK), CHUNK)

    loads = [
        pltpu.make_async_copy(start_r, pr.at[0], in_sem.at[0]),
        pltpu.make_async_copy(start_l, ql.at[0], in_sem.at[1]),
        pltpu.make_async_copy(coll_hbm, coll, in_sem.at[2]),
    ]
    for load in loads:
        load.start()
    halo[...] = jnp.zeros_like(halo)

    barrier = pltpu.get_barrier_semaphore()
    for k in range(1, n_vel):
        pl.semaphore_signal(
            barrier, inc=1, device_id=(space, (vel + k) % n_vel), device_id_type=MESH
        )

    def greet(k, _):
        pl.semaphore_signal(
            barrier, inc=1, device_id=((space + k) % n_space, vel), device_id_type=MESH
        )
        return 0

    lax.fori_loop(1, n_space, greet, 0)
    pl.semaphore_wait(barrier, n_vel - 1 + n_space - 1)

    def send(src, dst, ssem, rsem, target):
        return pltpu.make_async_remote_copy(
            src_ref=src, dst_ref=dst, send_sem=ssem, recv_sem=rsem,
            device_id=target, device_id_type=MESH,
        )

    lane = lax.broadcasted_iota(jnp.int32, (8, LANES), 1)
    line = lax.broadcasted_iota(jnp.int32, (8, LANES), 0)

    def to_tile(accs):
        tile = jnp.zeros((8, LANES), F32)
        for k, acc in enumerate(accs):
            total = jnp.sum(jnp.sum(acc, axis=0, keepdims=True), axis=1, keepdims=True)
            tile = jnp.where((lane == k) & (line == 0), total, tile)
        return tile

    def all_sum(tile, turn):
        slot = turn % 2
        red_own[slot] = tile
        red_vel[slot, vel] = tile
        first = []
        for k in range(1, n_vel):
            copy = send(
                red_own.at[slot], red_vel.at[slot, vel], v_send.at[slot, k], v_recv.at[slot, vel],
                (space, (vel + k) % n_vel),
            )
            copy.start()
            first.append(copy)
        for k in range(1, n_vel):
            other = (vel + k) % n_vel
            send(
                red_own.at[slot], red_vel.at[slot, other], v_send.at[slot, k],
                v_recv.at[slot, other], (space, other),
            ).wait_recv()
        for copy in first:
            copy.wait_send()
        mid = red_vel[slot, 0]
        for k in range(1, n_vel):
            mid = mid + red_vel[slot, k]
        red_mid[slot] = mid
        red_space[slot, space] = mid

        def to(k):
            other = (space + k) % n_space
            return send(
                red_mid.at[slot], red_space.at[slot, space], s_send.at[slot, k],
                s_recv.at[slot, space], (other, vel),
            )

        def go(k, _):
            to(k).start()
            return 0

        def arrive(k, _):
            other = (space + k) % n_space
            send(
                red_mid.at[slot], red_space.at[slot, other], s_send.at[slot, k],
                s_recv.at[slot, other], (other, vel),
            ).wait_recv()
            return 0

        def left(k, _):
            to(k).wait_send()
            return 0

        lax.fori_loop(1, n_space, go, 0)
        lax.fori_loop(1, n_space, arrive, 0)
        lax.fori_loop(1, n_space, left, 0)
        total = red_space[slot, 0]
        for k in range(1, n_space):
            total = total + red_space[slot, k]
        return total

    def pick(tile, k):
        return tile[0:1, k : k + 1]

    def fold(x):
        return jnp.sum(x.reshape(CHUNK // 8, 8, cells), axis=0)

    zero = jnp.zeros((8, cells), F32)
    loads[0].wait()
    loads[1].wait()

    def squares(c, accs):
        r, l = pr[0, at(c), :], ql[0, at(c), :]
        return (accs[0] + fold(r * r), accs[1] + fold(l * l))

    lengths_tile = to_tile(lax.fori_loop(0, steps, squares, (zero, zero)))

    inv_vol = 1.0 / vol_ref[...]
    freq = freq_ref[...]
    sixteen = lax.broadcasted_iota(jnp.int32, (16, cells), 0)
    high = inv_vol.astype(BF16).astype(F32)
    middle = (inv_vol - high).astype(BF16).astype(F32)
    low = inv_vol - high - middle
    ivp[...] = jnp.where(
        sixteen == 0, high, jnp.where(sixteen == 1, middle, jnp.where(sixteen == 2, low, 0.0))
    ).astype(BF16)
    for f in range(6):
        depth = gather.shape[1]
        source = lax.broadcasted_iota(jnp.int32, (depth, cells), 0)
        gather[f] = jnp.where(source == fn_ref[f : f + 1, :], 1.0, 0.0).astype(BF16)
    source = lax.broadcasted_iota(jnp.int32, (cells, 4 * face), 0)
    pack[...] = jnp.where(source == ss_ref[...], 1.0, 0.0).astype(BF16)
    corner = dot(ivp[...], pack[...]).astype(BF16)
    for g in range(4):
        hsend[g, 2 * rows : 2 * rows + 16, :] = corner[:, g * face : (g + 1) * face]

    def prepare(c, _):
        ids = vel * rows + c * CHUNK + lax.broadcasted_iota(jnp.int32, (CHUNK, cells), 0)
        total = jnp.zeros((CHUNK, cells), F32)
        for axis, index in enumerate((ids // (NV * NV), ids // NV % NV, ids % NV)):
            xi = (index.astype(F32) - (NV - 1) / 2.0) * (6.0 / NV)
            speed[axis, at(c), :] = xi
            total = total + jnp.maximum(-xi, 0.0) * fa_ref[2 * axis : 2 * axis + 1, :]
            total = total + jnp.maximum(xi, 0.0) * fa_ref[2 * axis + 1 : 2 * axis + 2, :]
        diag[at(c), :] = total * inv_vol
        return 0

    lax.fori_loop(0, steps, prepare, 0)
    loads[2].wait()

    def turn_over(c, _):
        for r in range(steps):
            block = coll[r * CHUNK : (r + 1) * CHUNK, at(c)]
            coll_t[at(c), r * CHUNK : (r + 1) * CHUNK] = block.T
        return 0

    lax.fori_loop(0, coll.shape[1] // CHUNK, turn_over, 0)
    lengths = all_sum(lengths_tile, 0)
    inv_r = 1.0 / jnp.sqrt(pick(lengths, 0) + EPSILON)
    inv_l = 1.0 / jnp.sqrt(pick(lengths, 1) + EPSILON)

    def scale(c, _):
        r, l = pr[0, at(c), :] * inv_r, ql[0, at(c), :] * inv_l
        pr[0, at(c), :] = r
        ql[0, at(c), :] = l
        wr[at(c), :] = r.astype(BF16)
        wl[0, at(c), :] = l.astype(BF16)
        return 0

    lax.fori_loop(0, steps, scale, 0)

    def leave(j):
        copies = [
            pltpu.make_async_copy(pr.at[j], right_out.at[j], out_sem.at[0, j]),
            pltpu.make_async_copy(ql.at[j], left_out.at[j], out_sem.at[1, j]),
        ]
        for copy in copies:
            copy.start()
        return copies

    outgoing = leave(0)
    gram = jnp.zeros((8, LANES), F32)
    right_hess = jnp.zeros((8, LANES), F32)
    left_hess = jnp.zeros((8, LANES), F32)

    def pairs(j):
        return [(j, k) for k in range(j + 1)] + [(i, j) for i in range(j)]

    def add_gram(gram, accs, j):
        for (i, k), acc in zip(pairs(j), accs):
            total = jnp.sum(jnp.sum(acc, axis=0, keepdims=True), axis=1, keepdims=True)
            place = i * (ITERS + 1) + k
            gram = jnp.where((lane == place) & (line == 0), total, gram)
        return gram

    def partial_sums(owner, c):
        start = pl.multiple_of(owner * rows + c * CHUNK, CHUNK)
        return dot(coll_t[pl.ds(start, CHUNK), :], wr[...])

    def adjoint_part(owner, slot, c):
        columns = pl.ds(pl.multiple_of(owner * rows, rows), rows)
        return dot(coll[at(c), columns], wl[slot])

    def halo_sends(started):
        for g in range(4):
            to, source = space + offsets[g], space - offsets[g]
            copy = send(
                hsend.at[g], halo.at[g], h_send.at[g], h_recv.at[g],
                ((to + n_space) % n_space, vel),
            )
            if started == "start":
                pl.when((to >= 0) & (to < n_space))(copy.start)
            elif started == "sent":
                pl.when((to >= 0) & (to < n_space))(copy.wait_send)
            else:
                pl.when((source >= 0) & (source < n_space))(copy.wait_recv)

    for j in range(ITERS):
        parts = [pl.ds(0, half), pl.ds(half, half)]
        across = [
            send(wl.at[0, p], wl.at[2, p], ag_send.at[h], ag_recv.at[h], (space, far))
            for h, p in enumerate(parts)
        ]
        beside = send(wl.at[0], wl.at[1], ag_send.at[2], ag_recv.at[2], (space, near))
        for copy in across:
            copy.start()
        beside.start()

        summed = []
        for slot, owner in ((1, diagonal), (0, near)):
            def product(c, _, slot=slot, owner=owner):
                rs_send[slot, at(c), :] = partial_sums(owner, c).astype(BF16)
                return 0

            lax.fori_loop(0, steps, product, 0)
            copy = send(
                rs_send.at[slot], rs_got.at[slot], rs_ssem.at[slot], rs_rsem.at[slot],
                (space, near),
            )
            copy.start()
            summed.append(copy)

        def packing(c, _):
            for t in range(2):
                vector = wr[at(c), :] if t == 0 else wl[0, at(c), :]
                out = dot(vector, pack[...]).astype(BF16)
                where = pl.ds(pl.multiple_of(t * rows + c * CHUNK, CHUNK), CHUNK)
                for g in range(4):
                    hsend[g, where, :] = out[:, g * face : (g + 1) * face]
            return 0

        lax.fori_loop(0, steps, packing, 0)
        halo_sends("start")

        def far_part(c, _):
            part[at(c), :] = partial_sums(far, c)
            return 0

        lax.fori_loop(0, steps, far_part, 0)
        summed[0].wait_recv()
        shipped = []
        for h, p in enumerate(parts):
            def joined(c, _):
                rs_xsend[at(c), :] = (part[at(c), :] + rs_got[1, at(c), :].astype(F32)).astype(BF16)
                return 0

            lax.fori_loop(h * (steps // 2), (h + 1) * (steps // 2), joined, 0)
            copy = send(
                rs_xsend.at[p], rs_xgot.at[p], rs_ssem.at[2 + h], rs_rsem.at[2 + h], (space, far)
            )
            copy.start()
            shipped.append(copy)

        def own_part(c, _):
            pr[j + 1, at(c), :] = partial_sums(vel, c)
            ql[j + 1, at(c), :] = adjoint_part(vel, 0, c)
            return 0

        lax.fori_loop(0, steps, own_part, 0)
        beside.wait_recv()
        summed[1].wait_recv()

        def near_part(c, _):
            pr[j + 1, at(c), :] = freq * (pr[j + 1, at(c), :] + rs_got[0, at(c), :].astype(F32))
            ql[j + 1, at(c), :] = ql[j + 1, at(c), :] + adjoint_part(near, 1, c)
            return 0

        lax.fori_loop(0, steps, near_part, 0)
        passed = []
        for h, p in enumerate(parts):
            across[h].wait_recv()
            copy = send(
                wl.at[2, p], wl.at[3, p], ag_send.at[3 + h], ag_recv.at[3 + h], (space, near)
            )
            copy.start()
            passed.append(copy)

        halo_sends("arrive")
        if j == 0:
            for f in range(6):
                known = jnp.concatenate(
                    [ivp[...]] + [halo[g, 2 * rows : 2 * rows + 16, :] for g in range(4)], axis=1
                )
                three = dot(known, gather[f])
                area_l[f : f + 1, :] = fa_ref[f : f + 1, :] * jnp.sum(
                    three, axis=0, keepdims=True
                )

        def transport(c, _):
            for t, basis in ((0, pr), (1, ql)):
                vector = wr[at(c), :] if t == 0 else wl[0, at(c), :]
                where = pl.ds(pl.multiple_of(t * rows + c * CHUNK, CHUNK), CHUNK)
                extended = jnp.concatenate(
                    [vector] + [halo[g, where, :] for g in range(4)], axis=1
                )
                out = diag[at(c), :] * vector.astype(F32)
                for f in range(6):
                    xi = speed[f // 2, at(c), :]
                    inward = xi if (f + t) % 2 == 1 else -xi
                    if t == 0:
                        weight = fa_ref[f : f + 1, :] * inv_vol
                    else:
                        weight = area_l[f : f + 1, :]
                    out = out + jnp.minimum(inward, 0.0) * (weight * dot(extended, gather[f]))
                if t == 0:
                    basis[j + 1, at(c), :] = basis[j + 1, at(c), :] + out
                else:
                    part[at(c), :] = out
            return 0

        lax.fori_loop(0, steps, transport, 0)

        def gram_step(c, accs):
            return tuple(
                acc + fold(ql[i, at(c), :] * pr[k, at(c), :])
                for (i, k), acc in zip(pairs(j), accs)
            )

        accs = lax.fori_loop(0, steps, gram_step, (zero,) * len(pairs(j)))
        gram = add_gram(gram, accs, j)

        for copy in passed:
            copy.wait_recv()

        def left_end(c, accs):
            total = ql[j + 1, at(c), :] + adjoint_part(far, 2, c) + adjoint_part(diagonal, 3, c)
            new = part[at(c), :] + freq * total
            ql[j + 1, at(c), :] = new
            return tuple(
                acc + fold(new * (ql[i, at(c), :] if i <= j else new))
                for i, acc in enumerate(accs)
            )

        left_dots = lax.fori_loop(0, steps, left_end, (zero,) * (j + 2))

        def right_end(c, accs):
            new = pr[j + 1, at(c), :] + freq * rs_xgot[at(c), :].astype(F32)
            pr[j + 1, at(c), :] = new
            return tuple(
                acc + fold(new * (pr[i, at(c), :] if i <= j else new))
                for i, acc in enumerate(accs)
            )

        right_dots = (zero,) * (j + 2)
        for h in range(2):
            shipped[h].wait_recv()
            right_dots = lax.fori_loop(
                h * (steps // 2), (h + 1) * (steps // 2), right_end, right_dots
            )
        for copy in across + [beside] + summed + shipped + passed:
            copy.wait_send()
        halo_sends("sent")

        sums = all_sum(to_tile(list(right_dots) + list(left_dots)), j + 1)
        right_coef = [pick(sums, i) for i in range(j + 1)]
        left_coef = [pick(sums, j + 2 + i) for i in range(j + 1)]
        right_raw, left_raw = pick(sums, j + 1), pick(sums, 2 * j + 3)
        for i in range(j + 1):
            right_raw = right_raw - right_coef[i] * right_coef[i]
            left_raw = left_raw - left_coef[i] * left_coef[i]
        right_norm = jnp.sqrt(right_raw + EPSILON)
        left_norm = jnp.sqrt(left_raw + EPSILON)
        for i in range(j + 2):
            here = (line == i) & (lane == j)
            right_hess = jnp.where(here, right_coef[i] if i <= j else right_norm, right_hess)
            left_hess = jnp.where(here, left_coef[i] if i <= j else left_norm, left_hess)
        inv_r, inv_l = 1.0 / right_norm, 1.0 / left_norm
        last = j == ITERS - 1

        def finish(c, accs):
            r, l = pr[j + 1, at(c), :], ql[j + 1, at(c), :]
            for i in range(j + 1):
                r = r - right_coef[i] * pr[i, at(c), :]
                l = l - left_coef[i] * ql[i, at(c), :]
            r, l = r * inv_r, l * inv_l
            pr[j + 1, at(c), :] = r
            ql[j + 1, at(c), :] = l
            if not last:
                wr[at(c), :] = r.astype(BF16)
                wl[0, at(c), :] = l.astype(BF16)
            return accs

        lax.fori_loop(0, steps, finish, 0)
        outgoing += leave(j + 1)

    def gram_last(c, accs):
        return tuple(
            acc + fold(ql[i, at(c), :] * pr[k, at(c), :])
            for (i, k), acc in zip(pairs(ITERS), accs)
        )

    accs = lax.fori_loop(0, steps, gram_last, (zero,) * len(pairs(ITERS)))
    total = all_sum(add_gram(gram, accs, ITERS), ITERS + 1)
    gram_tile = jnp.zeros((8, LANES), F32)
    for i in range(ITERS + 1):
        for k in range(ITERS + 1):
            gram_tile = jnp.where(
                (line == i) & (lane == k), pick(total, i * (ITERS + 1) + k), gram_tile
            )
    gram_out[...] = gram_tile[: ITERS + 1, : ITERS + 1]
    rh_out[...] = right_hess[: ITERS + 1, :ITERS]
    lh_out[...] = left_hess[: ITERS + 1, :ITERS]
    for copy in outgoing:
        copy.wait()


def per_device(
    start_right, start_left, collision, frequency, volume, face_neighbor, face_area, send_slot
):
    rows, cells = start_right.shape
    face = send_slot.shape[1]
    n_space, n_vel = lax.axis_size("space"), lax.axis_size("vel")
    assert n_vel == 4 and rows % (2 * CHUNK) == 0
    depth = cells + 4 * face
    tall = 2 * rows + 16
    vmem = pl.BlockSpec(memory_space=pltpu.VMEM)
    hbm = pl.BlockSpec(memory_space=pl.ANY)
    basis = jax.ShapeDtypeStruct((ITERS + 1, rows, cells), F32)
    hess = jax.ShapeDtypeStruct((ITERS + 1, ITERS), F32)
    dma = pltpu.SemaphoreType.DMA
    return pl.pallas_call(
        functools.partial(kernel, (n_space, n_vel, n_space // 4)),
        out_shape=(
            basis, basis, hess, hess, jax.ShapeDtypeStruct((ITERS + 1, ITERS + 1), F32)
        ),
        in_specs=[hbm] * 3 + [vmem] * 5,
        out_specs=(hbm, hbm, vmem, vmem, vmem),
        scratch_shapes=[
            pltpu.VMEM(collision.shape, BF16),
            pltpu.VMEM((collision.shape[1], rows), BF16),
            pltpu.VMEM((ITERS + 1, rows, cells), F32),
            pltpu.VMEM((ITERS + 1, rows, cells), F32),
            pltpu.VMEM((rows, cells), BF16),
            pltpu.VMEM((4, rows, cells), BF16),
            pltpu.VMEM((4, tall, face), BF16),
            pltpu.VMEM((4, tall, face), BF16),
            pltpu.VMEM((cells, 4 * face), BF16),
            pltpu.VMEM((6, depth, cells), BF16),
            pltpu.VMEM((16, cells), BF16),
            pltpu.VMEM((8, cells), F32),
            pltpu.VMEM((rows, cells), F32),
            pltpu.VMEM((3, rows, cells), F32),
            pltpu.VMEM((rows, cells), F32),
            pltpu.VMEM((2, rows, cells), BF16),
            pltpu.VMEM((2, rows, cells), BF16),
            pltpu.VMEM((rows, cells), BF16),
            pltpu.VMEM((rows, cells), BF16),
            pltpu.VMEM((2, 8, LANES), F32),
            pltpu.VMEM((2, n_vel, 8, LANES), F32),
            pltpu.VMEM((2, 8, LANES), F32),
            pltpu.VMEM((2, n_space, 8, LANES), F32),
            dma((3,)),
            dma((2, ITERS + 1)),
            dma((5,)),
            dma((5,)),
            dma((4,)),
            dma((4,)),
            dma((4,)),
            dma((4,)),
            dma((2, n_vel)),
            dma((2, n_vel)),
            dma((2, n_space)),
            dma((2, n_space)),
        ],
        compiler_params=pltpu.CompilerParams(
            collective_id=0, has_side_effects=True, vmem_limit_bytes=60 * 1024 * 1024
        ),
    )(
        start_right, start_left, collision, frequency.reshape(1, -1), volume.reshape(1, -1),
        face_neighbor, face_area, send_slot.reshape(1, -1),
    )


def solution(mesh):
    placed = (
        P("vel", "space"),
        P("vel", "space"),
        P("vel", None),
        P("space"),
        P("space"),
        P(None, "space"),
        P(None, "space"),
        P(None, "space"),
    )
    return jax.shard_map(
        per_device,
        mesh=mesh,
        in_specs=placed,
        out_specs=(P(None, "vel", "space"), P(None, "vel", "space"), P(), P(), P()),
        check_vma=False,
    )
```

time: 878 us -> 217 us (0.25); the launches traced: 866 us -> 217 us
  blocking collectives: 263 us -> 0 us
  local copies, waits for them, and re-layouts: 243 us -> 11.2 us
  Pallas kernels: 0 us -> 205 us
  other arithmetic: 123 us -> 0 us
  matrix products: 111 us -> 0 us
  starting transfers between devices: 58.5 us -> 0 us
  waiting for transfers between devices: 38.3 us -> 0 us
  between operations: 30.1 us -> 0.65 us
    psum x6 -> x0, blocking collectives: 263 us -> none  [the longest x4 181 us: per_device(): lax.psum((dots_right, dots_left, jnp.sum(right_new * right_new), jnp.sum(...]
    pallas_call x0 -> x1, Pallas kernels: none -> 205 us  [per_device(): pl.pallas_call(functools.partial(kernel, (n_space, n_vel, n_space // 4)),...]
    gather x90 -> x0, local copies, waits for them, and re-layouts: 190 us -> none  [the longest x24 47.5 us: per_device(): jnp.take(left_ext, face_neighbor[transport_facing], axis=1)]
    dot_general x9 -> x0, matrix products: 111 us -> none  [the longest x4 57.2 us: per_device(): jnp.dot(collision, lax.all_gather(left_w, 'vel', axis=0, tiled=True), pre...]
    ppermute x20 -> x0, starting transfers between devices: 57.7 us -> none  [from_behind(): return lax.ppermute(block, axis, route)]
    another operation x51 -> x0, other arithmetic: 56.4 us -> none  [the longest x32 17.2 us: per_device(): jnp.stack([jnp.take(right_w, send_slot[extended_direction], axis=1), jnp....]
    ppermute x20 -> x0, waiting for transfers between devices: 38.1 us -> none  [from_behind(): return lax.ppermute(block, axis, route)]
    unnamed x15 -> x0, other arithmetic: 36.5 us -> none
  transfers between devices with their start and end apart: 28 -> 0, of which waited for: 8 -> 0; matrix products, arithmetic and copies ran while one was open for 41% -> 0% of each run, Pallas kernels for 0% -> 0%
where the time goes in v1:
time: 217 us
  Pallas kernels  205 us (94%)
  local copies, waits for them, and re-layouts  11.2 us (5%)
    pallas_call x1, Pallas kernels, per_device(): pl.pallas_call(functools.partial(kernel, (n_space, n_vel, n_space // 4)),...  205 us
    unnamed x7, local copies, waits for them, and re-layouts  8.51 us

profile of v1, /device:TPU:0, one launch (start us, length us, event | category | flops | bytes accessed | tf_op | source)
XLA Modules:
  0.0 217.2 jit_solution(15641148603623029811)
XLA Ops:
  0.6 205.4 %shard_map.119 = (f32[5,1024,256]{2,1,0:T(8,128)}, f32[5,1024,256]{2,1,0:T(8,128)}, f32[5,4]{1,0:T(8,128)}, f32[5,4]{1,0:T(8,128)}, f32[5,5]{1,0:T(8,128)}) custom-call(f32[1024,256]{1,0:T(8,128)} %start_r.1, f32[1024,256]{1,0:T(8,128)} %start_l.1, bf16[1024,4096]{1,0:T(8,128)(2,1)} %coll_hbm.1, f32[1,256]{1,0:T(1,128)} %bitcast.4, f32[1,256]{1,0:T(1,128)} %bitcast.5, ...), custom_call_target="tpu_custom_call" | custom-call | tf_op jit(solution)/shard_map/pallas_call | solution.py:485
  206.0 1.3 copy.13
  207.4 1.3 copy.14
  208.7 0.0 copy-start
  208.7 5.6 %copy.18 = f32[5,1024,256]{2,1,0:T(8,128)} copy(f32[5,1024,256]{2,1,0:T(8,128)} %get-tuple-element.15) | data formatting | bytes 10485760
  214.3 0.0 copy-done
  214.3 0.0 copy-start.1
  214.3 2.4 %copy.19 = f32[5,1024,256]{2,1,0:T(8,128)} copy(f32[5,1024,256]{2,1,0:T(8,128)S(1)} %copy-done) | data formatting | bytes 10485760
  216.6 0.0 copy-done.1
  216.6 0.6 copy.20
Async XLA Ops:
  208.7 5.6 %copy-start = (f32[5,1024,256]{2,1,0:T(8,128)S(1)}, f32[5,1024,256]{2,1,0:T(8,128)}, u32[]{:S(2)}) copy-start(f32[5,1024,256]{2,1,0:T(8,128)} %get-tuple-element.16) | copy-start | bytes 15728644
  214.3 2.4 %copy-start.1 = (f32[5,5]{1,0:T(8,128)S(1)}, f32[5,5]{1,0:T(8,128)}, u32[]{:S(2)}) copy-start(f32[5,5]{1,0:T(8,128)} %get-tuple-element.19) | copy-start | bytes 304

commit v2 on v1

--- a/solution.py
+++ b/solution.py
@@ -11,7 +11,7 @@
 ITERS = 4
 EPSILON = 1e-06
 LANES = 128
-CHUNK = 256
+CHUNK = NV * NV
 MESH = pl.DeviceIdType.MESH
 F32 = jnp.float32
 BF16 = jnp.bfloat16
@@ -25,7 +25,7 @@
     sizes, start_r, start_l, coll_hbm, freq_ref, vol_ref, fn_ref, fa_ref, ss_ref,
     right_out, left_out, rh_out, lh_out, gram_out,
     coll, coll_t, pr, ql, wr, wl, hsend, halo, pack, gather, ivp, area_l,
-    diag, speed, part, rs_send, rs_got, rs_xsend, rs_xgot,
+    diag, coef, part, rs_send, rs_got, rs_xsend, rs_xgot,
     red_own, red_vel, red_mid, red_space,
     in_sem, out_sem, ag_send, ag_recv, rs_ssem, rs_rsem, h_send, h_recv,
     v_send, v_recv, s_send, s_recv,
@@ -104,8 +104,6 @@
                 red_own.at[slot], red_vel.at[slot, other], v_send.at[slot, k],
                 v_recv.at[slot, other], (space, other),
             ).wait_recv()
-        for copy in first:
-            copy.wait_send()
         mid = red_vel[slot, 0]
         for k in range(1, n_vel):
             mid = mid + red_vel[slot, k]
@@ -137,6 +135,8 @@
 
         lax.fori_loop(1, n_space, go, 0)
         lax.fori_loop(1, n_space, arrive, 0)
+        for copy in first:
+            copy.wait_send()
         lax.fori_loop(1, n_space, left, 0)
         total = red_space[slot, 0]
         for k in range(1, n_space):
@@ -169,9 +169,10 @@
         sixteen == 0, high, jnp.where(sixteen == 1, middle, jnp.where(sixteen == 2, low, 0.0))
     ).astype(BF16)
     for f in range(6):
-        depth = gather.shape[1]
-        source = lax.broadcasted_iota(jnp.int32, (depth, cells), 0)
-        gather[f] = jnp.where(source == fn_ref[f : f + 1, :], 1.0, 0.0).astype(BF16)
+        source = lax.broadcasted_iota(jnp.int32, (gather.shape[0], cells), 0)
+        gather[:, f * cells : (f + 1) * cells] = jnp.where(
+            source == fn_ref[f : f + 1, :], 1.0, 0.0
+        ).astype(BF16)
     source = lax.broadcasted_iota(jnp.int32, (cells, 4 * face), 0)
     pack[...] = jnp.where(source == ss_ref[...], 1.0, 0.0).astype(BF16)
     corner = dot(ivp[...], pack[...]).astype(BF16)
@@ -183,7 +184,6 @@
         total = jnp.zeros((CHUNK, cells), F32)
         for axis, index in enumerate((ids // (NV * NV), ids // NV % NV, ids % NV)):
             xi = (index.astype(F32) - (NV - 1) / 2.0) * (6.0 / NV)
-            speed[axis, at(c), :] = xi
             total = total + jnp.maximum(-xi, 0.0) * fa_ref[2 * axis : 2 * axis + 1, :]
             total = total + jnp.maximum(xi, 0.0) * fa_ref[2 * axis + 1 : 2 * axis + 2, :]
         diag[at(c), :] = total * inv_vol
@@ -247,17 +247,20 @@
 
     def halo_sends(started):
         for g in range(4):
-            to, source = space + offsets[g], space - offsets[g]
+            to = space + offsets[g]
+            place, extent = (space, n_space) if g < 2 else (space % row_blocks, row_blocks)
+            goes = (place + offsets[g] >= 0) & (place + offsets[g] < extent)
+            comes = (place - offsets[g] >= 0) & (place - offsets[g] < extent)
             copy = send(
                 hsend.at[g], halo.at[g], h_send.at[g], h_recv.at[g],
                 ((to + n_space) % n_space, vel),
             )
             if started == "start":
-                pl.when((to >= 0) & (to < n_space))(copy.start)
+                pl.when(goes)(copy.start)
             elif started == "sent":
-                pl.when((to >= 0) & (to < n_space))(copy.wait_send)
+                pl.when(goes)(copy.wait_send)
             else:
-                pl.when((source >= 0) & (source < n_space))(copy.wait_recv)
+                pl.when(comes)(copy.wait_recv)
 
     for j in range(ITERS):
         parts = [pl.ds(0, half), pl.ds(half, half)]
@@ -345,10 +348,27 @@
                 known = jnp.concatenate(
                     [ivp[...]] + [halo[g, 2 * rows : 2 * rows + 16, :] for g in range(4)], axis=1
                 )
-                three = dot(known, gather[f])
+                three = dot(known, gather[:, f * cells : (f + 1) * cells])
                 area_l[f : f + 1, :] = fa_ref[f : f + 1, :] * jnp.sum(
                     three, axis=0, keepdims=True
                 )
+
+            def weights(c, _):
+                ids = vel * rows + c * CHUNK + lax.broadcasted_iota(jnp.int32, (CHUNK, cells), 0)
+                for axis, index in enumerate((ids // (NV * NV), ids // NV % NV, ids % NV)):
+                    xi = (index.astype(F32) - (NV - 1) / 2.0) * (6.0 / NV)
+                    low, high = slice(2 * axis, 2 * axis + 1), slice(2 * axis + 1, 2 * axis + 2)
+                    coef[0, axis, at(c), :] = inv_vol * (
+                        jnp.minimum(-xi, 0.0) * fa_ref[low, :]
+                        + jnp.minimum(xi, 0.0) * fa_ref[high, :]
+                    )
+                    coef[1, axis, at(c), :] = (
+                        jnp.minimum(xi, 0.0) * area_l[low, :]
+                        + jnp.minimum(-xi, 0.0) * area_l[high, :]
+                    )
+                return 0
+
+            lax.fori_loop(0, steps, weights, 0)
 
         def transport(c, _):
             for t, basis in ((0, pr), (1, ql)):
@@ -357,15 +377,29 @@
                 extended = jnp.concatenate(
                     [vector] + [halo[g, where, :] for g in range(4)], axis=1
                 )
+                plane = (vel * rows + c * CHUNK) // (NV * NV)
+                side = (plane // (NV // 2) + 1 + t) % 2
+                along_x = pl.ds(pl.multiple_of(side * cells, cells), cells)
+                got_x = dot(extended, gather[:, along_x])
+                first = 3 if t == 0 else 2
+                got_y = jnp.concatenate(
+                    [
+                        dot(extended[: CHUNK // 2], gather[:, first * cells : (first + 1) * cells]),
+                        dot(extended[CHUNK // 2 :], gather[:, (5 - first) * cells : (6 - first) * cells]),
+                    ],
+                    axis=0,
+                )
+                both = dot(extended, gather[:, 4 * cells :])
+                tiles = both.reshape(CHUNK // NV, 2, NV // 2, 2 * cells)
+                one, two = tiles[:, 0], tiles[:, 1]
+                below, above = (one[..., cells:], two[..., :cells])
+                if t == 1:
+                    below, above = (one[..., :cells], two[..., cells:])
+                got_z = jnp.stack([below, above], axis=1).reshape(CHUNK, cells)
                 out = diag[at(c), :] * vector.astype(F32)
-                for f in range(6):
-                    xi = speed[f // 2, at(c), :]
-                    inward = xi if (f + t) % 2 == 1 else -xi
-                    if t == 0:
-                        weight = fa_ref[f : f + 1, :] * inv_vol
-                    else:
-                        weight = area_l[f : f + 1, :]
-                    out = out + jnp.minimum(inward, 0.0) * (weight * dot(extended, gather[f]))
+                out = out + coef[t, 0, at(c), :] * got_x
+                out = out + coef[t, 1, at(c), :] * got_y
+                out = out + coef[t, 2, at(c), :] * got_z
                 if t == 0:
                     basis[j + 1, at(c), :] = basis[j + 1, at(c), :] + out
                 else:
@@ -499,11 +533,11 @@
             pltpu.VMEM((4, tall, face), BF16),
             pltpu.VMEM((4, tall, face), BF16),
             pltpu.VMEM((cells, 4 * face), BF16),
-            pltpu.VMEM((6, depth, cells), BF16),
+            pltpu.VMEM((depth, 6 * cells), BF16),
             pltpu.VMEM((16, cells), BF16),
             pltpu.VMEM((8, cells), F32),
             pltpu.VMEM((rows, cells), F32),
-            pltpu.VMEM((3, rows, cells), F32),
+            pltpu.VMEM((2, 3, rows, cells), F32),
             pltpu.VMEM((rows, cells), F32),
             pltpu.VMEM((2, rows, cells), BF16),
             pltpu.VMEM((2, rows, cells), BF16),

time: 217 us -> 170 us (0.78)
  Pallas kernels: 205 us -> 157 us
    pallas_call x1, Pallas kernels: 205 us -> 157 us  [per_device(): pl.pallas_call(functools.partial(kernel, (n_space, n_vel, n_space // 4)),...]
where the time goes in v2:
time: 170 us; the launch traced here: 169 us
  Pallas kernels  157 us (92%)
  local copies, waits for them, and re-layouts  11.2 us (7%)
    pallas_call x1, Pallas kernels, per_device(): pl.pallas_call(functools.partial(kernel, (n_space, n_vel, n_space // 4)),...  157 us
    unnamed x7, local copies, waits for them, and re-layouts  8.51 us

profile of v2, /device:TPU:0, one launch (start us, length us, event | category | flops | bytes accessed | tf_op | source)
XLA Modules:
  0.0 169.3 jit_solution(12182019205127893307)
XLA Ops:
  0.6 157.5 %shard_map.119 = (f32[5,1024,256]{2,1,0:T(8,128)}, f32[5,1024,256]{2,1,0:T(8,128)}, f32[5,4]{1,0:T(8,128)}, f32[5,4]{1,0:T(8,128)}, f32[5,5]{1,0:T(8,128)}) custom-call(f32[1024,256]{1,0:T(8,128)} %start_r.1, f32[1024,256]{1,0:T(8,128)} %start_l.1, bf16[1024,4096]{1,0:T(8,128)(2,1)} %coll_hbm.1, f32[1,256]{1,0:T(1,128)} %bitcast.4, f32[1,256]{1,0:T(1,128)} %bitcast.5, ...), custom_call_target="tpu_custom_call" | custom-call | tf_op jit(solution)/shard_map/pallas_call | solution.py:519
  158.1 1.3 copy.13
  159.5 1.3 copy.14
  160.8 0.0 copy-start
  160.8 5.6 %copy.18 = f32[5,1024,256]{2,1,0:T(8,128)} copy(f32[5,1024,256]{2,1,0:T(8,128)} %get-tuple-element.15) | data formatting | bytes 10485760
  166.3 0.0 copy-done
  166.3 0.0 copy-start.1
  166.3 2.4 %copy.19 = f32[5,1024,256]{2,1,0:T(8,128)} copy(f32[5,1024,256]{2,1,0:T(8,128)S(1)} %copy-done) | data formatting | bytes 10485760
  168.7 0.0 copy-done.1
  168.7 0.6 copy.20
Async XLA Ops:
  160.8 5.6 %copy-start = (f32[5,1024,256]{2,1,0:T(8,128)S(1)}, f32[5,1024,256]{2,1,0:T(8,128)}, u32[]{:S(2)}) copy-start(f32[5,1024,256]{2,1,0:T(8,128)} %get-tuple-element.16) | copy-start | bytes 15728644
  166.3 2.4 %copy-start.1 = (f32[5,5]{1,0:T(8,128)S(1)}, f32[5,5]{1,0:T(8,128)}, u32[]{:S(2)}) copy-start(f32[5,5]{1,0:T(8,128)} %get-tuple-element.19) | copy-start | bytes 304
